TPU v7x, 128 devices: a whole 4x4x4 slice. The times are simulated.
128 devices in a mesh: cluster: 8 (over z, x_hi), dp: 16 (over y, x_lo, core).
Axes of the slice: x: 4 (x_hi: 2, x_lo: 2; x = x_hi * 2 + x_lo), y: 4, z: 4, core: 2. Of those that a mesh axis runs over, the one named last changes fastest.
Arguments:
- documents: bfloat16 [32768, 1024], P('dp', 'cluster'), may hold values from -64 to 64
- centroids: bfloat16 [16384, 1024], P('cluster'), may hold values from -8 to 8
- domain_mass: float32 [32768, 256], P('dp'), may hold values from 0.01 to 10
Outputs:
- lift: float32 [16384, 256], P(('cluster', 'dp'))
- information: float32 [], replicated
All inputs are finite; a program needn't handle non-finite values.
Results may differ from a plain program's by a relative error of at most 0.0013.
Values may be sent and summed in bfloat16 or wider, within the bound.
A program may use at most 128 MiB of HBM per device.

v0:
```python
import math
import jax
import jax.numpy as jnp
from jax import lax
from jax.sharding import PartitionSpec as P

E = 1024


def shards(documents, centroids, domain_mass):
    scale = 3.0 / math.sqrt(E)
    doc_rows = documents.shape[0]
    local_k = centroids.shape[0]
    docs_total = doc_rows * lax.axis_size("dp")
    own_rows = local_k // lax.axis_size("dp")
    columns = centroids
    scores = (
        lax.dot_general(
            lax.all_gather(documents, "cluster", axis=1, tiled=True),
            columns,
            (((1,), (1,)), ((), ())),
            preferred_element_type=jnp.float32,
        )
        * scale
    )
    row_max = lax.pmax(jnp.max(scores, axis=1), "cluster")
    expo = jnp.exp(scores - row_max[:, None])
    row_total = lax.psum(jnp.sum(expo, axis=1), "cluster")
    assign = (expo / row_total[:, None]).astype(jnp.bfloat16)
    shares = (domain_mass / jnp.sum(domain_mass, axis=1, keepdims=True)).astype(jnp.bfloat16)
    columns = assign
    whole = lax.psum(
        lax.dot_general(
            columns, shares, (((0,), (0,)), ((), ())), preferred_element_type=jnp.float32
        ),
        "dp",
    )
    summed = lax.dynamic_slice_in_dim(whole, lax.axis_index("dp") * own_rows, own_rows, 0)
    joint = summed / docs_total
    cluster_mass = jnp.sum(joint, axis=1)
    domain_prior = lax.psum(jnp.sum(joint, axis=0), ("cluster", "dp"))
    lift = joint / (cluster_mass[:, None] * domain_prior[None, :])
    information = lax.psum(jnp.sum(joint * jnp.log(lift)), ("cluster", "dp"))
    return (lift, information)


def solution(mesh):
    return jax.shard_map(
        shards,
        mesh=mesh,
        in_specs=(P("dp", "cluster"), P("cluster", None), P("dp", None)),
        out_specs=(P(("cluster", "dp"), None), P()),
        check_vma=False,
    )
```

profile of v0, /device:TPU:1, one launch (start us, length us, event | category | flops | bytes accessed | tf_op | source)
XLA Modules:
  0.0 423.9 jit_solution(605599507388424641)
XLA Ops:
  7.2 0.0 all-gather.2.cloned.1.call-start
  7.2 0.7 all-gather.2.cloned.1.call-update
  7.9 0.0 all-reduce.2.cloned.1.call-start
  7.9 1.9 reduce_sum.46
  9.9 77.0 %all-gather.2.cloned.1.call-done = bf16[2048,1024]{1,0:T(8,128)(2,1)} async-done(((bf16[2048,128]{1,0:T(8,128)(2,1)}), bf16[2048,1024]{1,0:T(8,128)(2,1)}) %all-gather.2.cloned.1.call-update) | async-done | bytes 4194320 | tf_op jit(solution)/shard_map/all_gather | solution.py:19
  86.9 15.1 %multiply_reduce_fusion = (f32[2048]{0:T(1024)S(1)}, f32[2048,2048]{0,1:T(8,128)}) fusion(bf16[2048,1024]{1,0:T(8,128)(2,1)} %all-gather.2.cloned.1.call-done, bf16[2048,1024]{1,0:T(8,128)(2,1)} %param.4), kind=kOutput, calls=%fused_computation.2 | convolution fusion | flops 8598321152 | bytes 25174016 | tf_op jit(solution)/shard_map/dot_general | solution.py:18
  102.0 16.6 %pmax.7 = f32[2048]{0:T(1024)S(1)} all-reduce(f32[2048]{0:T(1024)S(1)} %get-tuple-element.6), channel_id=1, replica_groups=mesh['cluster'=8,'dp'=16] {'cluster'}, use_global_device_ids=true, to_apply=%region_1.0 | all-reduce | flops 2048 | bytes 16384 | tf_op jit(solution)/shard_map/pmax | solution.py:26
  118.6 0.0 copy-start
  118.6 8.7 %fusion = f32[2048]{0:T(1024)S(1)} fusion(f32[2048,2048]{0,1:T(8,128)} %get-tuple-element.7, f32[2048]{0:T(1024)S(1)} %pmax.7), kind=kLoop, calls=%fused_computation.3 | loop fusion | flops 12580864 | bytes 16793600 | tf_op jit(solution)/shard_map/reduce_sum | solution.py:28
  127.3 18.2 %psum.28 = f32[2048]{0:T(1024)S(1)} all-reduce(f32[2048]{0:T(1024)S(1)} %fusion), channel_id=1, replica_groups=mesh['cluster'=8,'dp'=16] {'cluster'}, use_global_device_ids=true, to_apply=%region_3.0 | all-reduce | flops 2048 | bytes 16384 | tf_op jit(solution)/shard_map/psum | solution.py:28
  145.5 0.0 copy-done
  145.5 9.1 %fusion.1 = f32[2048,256]{1,0:T(8,128)} fusion(f32[2048,2048]{0,1:T(8,128)} %get-tuple-element.7, f32[2048]{0:T(1024)S(1)} %psum.28, f32[2048]{0:T(1024)S(1)} %pmax.7, f32[2048,256]{1,0:T(8,128)S(1)} %copy-done, f32[2048]{0:T(1024)S(1)} %reduce_sum.46), kind=kOutput, calls=%fused_computation.4 | convolution fusion | flops 2165309440 | bytes 20996096 | tf_op jit(solution)/shard_map/dot_general | solution.py:33
  154.6 0.0 all-reduce.2.cloned.1.call-update
  154.7 129.3 %all-reduce.2.cloned.1.call-done = f32[2048,256]{1,0:T(8,128)} async-done(((f32[2048,256]{1,0:T(8,128)}), f32[2048,256]{1,0:T(8,128)}) %all-reduce.2.cloned.1.call-update) | async-done | bytes 2097168 | tf_op jit(solution)/shard_map/psum | solution.py:32
  283.9 1.0 fusion.4
  284.9 67.3 %psum.30 = f32[256]{0:T(256)S(1)} all-reduce(f32[256]{0:T(256)S(1)} %get-tuple-element.3), channel_id=1, replica_groups=mesh['cluster'=8,'dp'=16] {'cluster','dp'}, use_global_device_ids=true, to_apply=%region_8.0 | all-reduce | flops 256 | bytes 2048 | tf_op jit(solution)/shard_map/psum | solution.py:41
  352.2 2.3 multiply_reduce_fusion.1
  354.5 62.6 %psum.31 = f32[]{:T(128)} all-reduce(f32[]{:T(128)} %get-tuple-element.4), channel_id=1, replica_groups=mesh['cluster'=8,'dp'=16] {'cluster','dp'}, use_global_device_ids=true, to_apply=%region_10.0 | all-reduce | flops 1 | bytes 8 | tf_op jit(solution)/shard_map/psum | solution.py:43
Async XLA Ops:
  7.2 79.7 %all-gather.2.cloned.1.call-start = ((), (), s32[]{:S(2)}) async-start(), calls=%async_computation | async-start | bytes 4718592 | tf_op jit(solution)/shard_map/all_gather | solution.py:19
  7.9 276.0 %all-reduce.2.cloned.1.call-start = ((), (), s32[]{:S(2)}) async-start(), calls=%async_computation.1 | async-start | bytes 4194304 | tf_op jit(solution)/shard_map/psum | solution.py:32
  118.6 26.9 %copy-start = (f32[2048,256]{1,0:T(8,128)S(1)}, f32[2048,256]{1,0:T(8,128)}, u32[]{:S(2)}) copy-start(f32[2048,256]{1,0:T(8,128)} %param.5) | copy-start | bytes 6291460
Sparse Core Ops, SparseCore 0:
  10.2 76.6 all-gather.1
  154.8 129.0 all-reduce.1
where the time goes:
time: 424 us
  waiting for transfers between devices  207 us (49%)
  blocking collectives  165 us (39%)
  matrix products  24.2 us (6%)
  between operations  14.1 us (3%)
  other arithmetic  13.9 us (3%)
    psum x1, waiting for transfers between devices, shards(): lax.psum(lax.dot_general(columns, shares, (((0,), (0,)), ((), ())), prefe...  129 us
    all_gather x1, waiting for transfers between devices, shards(): lax.all_gather(documents, 'cluster', axis=1, tiled=True)  77 us
    psum x1, blocking collectives, shards(): domain_prior = lax.psum(jnp.sum(joint, axis=0), ('cluster', 'dp'))  67.3 us
    psum x1, blocking collectives, shards(): information = lax.psum(jnp.sum(joint * jnp.log(lift)), ('cluster', 'dp'))  62.6 us
    psum x1, blocking collectives, shards(): row_total = lax.psum(jnp.sum(expo, axis=1), 'cluster')  18.2 us
    pmax x1, blocking collectives, shards(): row_max = lax.pmax(jnp.max(scores, axis=1), 'cluster')  16.6 us
    dot_general x1, matrix products, shards(): lax.dot_general(lax.all_gather(documents, 'cluster', axis=1, tiled=True),...  15.1 us
    dot_general x1, matrix products, shards(): lax.dot_general(columns, shares, (((0,), (0,)), ((), ())), preferred_elem...  9.11 us
  transfers between devices with their start and end apart: 2, of which 2 were waited for; matrix products, arithmetic and copies ran while one was open for 0% of the time, Pallas kernels for 0%

commit v1 on v0

--- a/solution.py
+++ b/solution.py
@@ -29,11 +29,14 @@
     assign = (expo / row_total[:, None]).astype(jnp.bfloat16)
     shares = (domain_mass / jnp.sum(domain_mass, axis=1, keepdims=True)).astype(jnp.bfloat16)
     columns = assign
-    whole = lax.psum(
-        lax.dot_general(
-            columns, shares, (((0,), (0,)), ((), ())), preferred_element_type=jnp.float32
+    whole = jnp.sum(
+        lax.all_gather(
+            lax.dot_general(
+                columns, shares, (((0,), (0,)), ((), ())), preferred_element_type=jnp.float32
+            ),
+            "dp",
         ),
-        "dp",
+        axis=0,
     )
     summed = lax.dynamic_slice_in_dim(whole, lax.axis_index("dp") * own_rows, own_rows, 0)
     joint = summed / docs_total

time: 424 us -> 480 us (1.13)
  waiting for transfers between devices: 207 us -> 254 us
  other arithmetic: 13.9 us -> 24 us
    all_gather x0 -> x1, waiting for transfers between devices: none -> 176 us  [shards(): lax.all_gather(lax.dot_general(columns, shares, (((0,), (0,)), ((), ())),...]
    psum x1 -> x0, waiting for transfers between devices: 129 us -> none  [shards(): lax.psum(lax.dot_general(columns, shares, (((0,), (0,)), ((), ())), prefe...]
    reduce_sum x0 -> x1, other arithmetic: none -> 12.1 us  [shards(): jnp.sum(lax.all_gather(lax.dot_general(columns, shares, (((0,), (0,)), ((...]
where the time goes in v1:
time: 480 us
  waiting for transfers between devices  254 us (53%)
  blocking collectives  163 us (34%)
  matrix products  24.2 us (5%)
  other arithmetic  24 us (5%)
  between operations  14.1 us (3%)
    all_gather x1, waiting for transfers between devices, shards(): lax.all_gather(lax.dot_general(columns, shares, (((0,), (0,)), ((), ())),...  176 us
    all_gather x1, waiting for transfers between devices, shards(): lax.all_gather(documents, 'cluster', axis=1, tiled=True)  77 us
    psum x1, blocking collectives, shards(): domain_prior = lax.psum(jnp.sum(joint, axis=0), ('cluster', 'dp'))  65.9 us
    psum x1, blocking collectives, shards(): information = lax.psum(jnp.sum(joint * jnp.log(lift)), ('cluster', 'dp'))  62.6 us
    psum x1, blocking collectives, shards(): row_total = lax.psum(jnp.sum(expo, axis=1), 'cluster')  18.2 us
    pmax x1, blocking collectives, shards(): row_max = lax.pmax(jnp.max(scores, axis=1), 'cluster')  16.7 us
    dot_general x1, matrix products, shards(): lax.dot_general(lax.all_gather(documents, 'cluster', axis=1, tiled=True),...  15.1 us
    reduce_sum x1, other arithmetic, shards(): jnp.sum(lax.all_gather(lax.dot_general(columns, shares, (((0,), (0,)), ((...  12.1 us
  transfers between devices with their start and end apart: 2, of which 2 were waited for; matrix products, arithmetic and copies ran while one was open for 0% of the time, Pallas kernels for 0%

profile of v1, /device:TPU:1, one launch (start us, length us, event | category | flops | bytes accessed | tf_op | source)
XLA Modules:
  0.0 479.6 jit_solution(17093495844632664655)
XLA Ops:
  7.2 0.0 all-gather.4.cloned.1.call-start
  7.2 0.7 all-gather.4.cloned.1.call-update
  7.9 0.0 all-gather.6.cloned.1.call-start
  7.9 1.9 reduce_sum.55
  9.9 77.0 %all-gather.4.cloned.1.call-done = bf16[2048,1024]{1,0:T(8,128)(2,1)} async-done(((bf16[2048,128]{1,0:T(8,128)(2,1)}), bf16[2048,1024]{1,0:T(8,128)(2,1)}) %all-gather.4.cloned.1.call-update) | async-done | bytes 4194320 | tf_op jit(solution)/shard_map/all_gather | solution.py:19
  86.9 15.1 %multiply_reduce_fusion = (f32[2048]{0:T(1024)S(1)}, f32[2048,2048]{0,1:T(8,128)}) fusion(bf16[2048,1024]{1,0:T(8,128)(2,1)} %all-gather.4.cloned.1.call-done, bf16[2048,1024]{1,0:T(8,128)(2,1)} %param.4), kind=kOutput, calls=%fused_computation.2 | convolution fusion | flops 8598321152 | bytes 25174016 | tf_op jit(solution)/shard_map/dot_general | solution.py:18
  102.0 0.0 copy-start
  102.0 16.7 %pmax.7 = f32[2048]{0:T(1024)S(1)} all-reduce(f32[2048]{0:T(1024)S(1)} %get-tuple-element.6), channel_id=1, replica_groups=mesh['cluster'=8,'dp'=16] {'cluster'}, use_global_device_ids=true, to_apply=%region_1.0 | all-reduce | flops 2048 | bytes 16384 | tf_op jit(solution)/shard_map/pmax | solution.py:26
  118.7 8.6 %fusion = f32[2048]{0:T(1024)S(1)} fusion(f32[2048,2048]{0,1:T(8,128)} %get-tuple-element.7, f32[2048]{0:T(1024)S(1)} %pmax.7), kind=kLoop, calls=%fused_computation.3 | loop fusion | flops 12580864 | bytes 16793600 | tf_op jit(solution)/shard_map/reduce_sum | solution.py:28
  127.3 18.2 %psum.21 = f32[2048]{0:T(1024)S(1)} all-reduce(f32[2048]{0:T(1024)S(1)} %fusion), channel_id=1, replica_groups=mesh['cluster'=8,'dp'=16] {'cluster'}, use_global_device_ids=true, to_apply=%region_3.0 | all-reduce | flops 2048 | bytes 16384 | tf_op jit(solution)/shard_map/psum | solution.py:28
  145.5 0.0 copy-done
  145.5 9.1 %fusion.1 = f32[2048,256]{1,0:T(8,128)} fusion(f32[2048,2048]{0,1:T(8,128)} %get-tuple-element.7, f32[2048]{0:T(1024)S(1)} %psum.21, f32[2048]{0:T(1024)S(1)} %pmax.7, f32[2048,256]{1,0:T(8,128)S(1)} %copy-done, f32[2048]{0:T(1024)S(1)} %reduce_sum.55), kind=kOutput, calls=%fused_computation.4 | convolution fusion | flops 2165309440 | bytes 20996096 | tf_op jit(solution)/shard_map/dot_general | solution.py:34
  154.6 0.0 all-gather.6.cloned.1.call-update
  154.6 176.1 %all-gather.6.cloned.1.call-done = f32[32768,256]{1,0:T(8,128)} async-done(((f32[2048,256]{1,0:T(8,128)}), f32[32768,256]{1,0:T(8,128)}) %all-gather.6.cloned.1.call-update) | async-done | bytes 33554448 | tf_op jit(solution)/shard_map/all_gather | solution.py:33
  330.7 12.1 %reduce_sum.56 = f32[2048,256]{1,0:T(8,128)S(1)} reduce(f32[16,2048,256]{2,1,0:T(8,128)} %bitcast.3, f32[]{:T(128)} %constant.3.clone.1), dimensions={0}, to_apply=%region_5.0 | reduce | flops 7864320 | bytes 35651588 | tf_op jit(solution)/shard_map/reduce_sum | solution.py:32
  342.8 0.1 fusion.4
  342.9 65.9 %psum.22 = f32[256]{0:T(256)S(1)} all-reduce(f32[256]{0:T(256)S(1)} %get-tuple-element.3), channel_id=1, replica_groups=mesh['cluster'=8,'dp'=16] {'cluster','dp'}, use_global_device_ids=true, to_apply=%region_8.0 | all-reduce | flops 256 | bytes 2048 | tf_op jit(solution)/shard_map/psum | solution.py:44
  408.8 1.4 multiply_reduce_fusion.1
  410.1 62.6 %psum.23 = f32[]{:T(128)} all-reduce(f32[]{:T(128)} %get-tuple-element.4), channel_id=1, replica_groups=mesh['cluster'=8,'dp'=16] {'cluster','dp'}, use_global_device_ids=true, to_apply=%region_10.0 | all-reduce | flops 1 | bytes 8 | tf_op jit(solution)/shard_map/psum | solution.py:46
Async XLA Ops:
  7.2 79.7 %all-gather.4.cloned.1.call-start = ((), (), s32[]{:S(2)}) async-start(), calls=%async_computation | async-start | bytes 4718592 | tf_op jit(solution)/shard_map/all_gather | solution.py:19
  7.9 322.8 %all-gather.6.cloned.1.call-start = ((), (), s32[]{:S(2)}) async-start(), calls=%async_computation.1 | async-start | bytes 35651584 | tf_op jit(solution)/shard_map/all_gather | solution.py:33
  102.0 43.5 %copy-start = (f32[2048,256]{1,0:T(8,128)S(1)}, f32[2048,256]{1,0:T(8,128)}, u32[]{:S(2)}) copy-start(f32[2048,256]{1,0:T(8,128)} %param.5) | copy-start | bytes 6291460
Sparse Core Ops, SparseCore 0:
  10.2 76.6 all-gather.3
  154.7 175.9 all-gather.5

commit v2 on v0

--- a/solution.py
+++ b/solution.py
@@ -38,7 +38,7 @@
     summed = lax.dynamic_slice_in_dim(whole, lax.axis_index("dp") * own_rows, own_rows, 0)
     joint = summed / docs_total
     cluster_mass = jnp.sum(joint, axis=1)
-    domain_prior = lax.psum(jnp.sum(joint, axis=0), ("cluster", "dp"))
+    domain_prior = lax.psum(lax.psum(jnp.sum(joint, axis=0), "cluster"), "dp")
     lift = joint / (cluster_mass[:, None] * domain_prior[None, :])
     information = lax.psum(jnp.sum(joint * jnp.log(lift)), ("cluster", "dp"))
     return (lift, information)

time: 424 us -> 409 us (0.965)
  blocking collectives: 165 us -> 149 us
    psum x1 -> x2, blocking collectives: 67.3 us -> 52.4 us  [shards(): domain_prior = lax.psum(lax.psum(jnp.sum(joint, axis=0), 'cluster'), 'dp')]
where the time goes in v2:
time: 409 us; the launch traced here: 408 us
  waiting for transfers between devices  207 us (51%)
  blocking collectives  149 us (36%)
  matrix products  24.2 us (6%)
  between operations  14.1 us (3%)
  other arithmetic  13.9 us (3%)
    psum x1, waiting for transfers between devices, shards(): lax.psum(lax.dot_general(columns, shares, (((0,), (0,)), ((), ())), prefe...  129 us
    all_gather x1, waiting for transfers between devices, shards(): lax.all_gather(documents, 'cluster', axis=1, tiled=True)  77 us
    psum x1, blocking collectives, shards(): information = lax.psum(jnp.sum(joint * jnp.log(lift)), ('cluster', 'dp'))  62 us
    psum x2, blocking collectives, shards(): domain_prior = lax.psum(lax.psum(jnp.sum(joint, axis=0), 'cluster'), 'dp')  52.4 us
    psum x1, blocking collectives, shards(): row_total = lax.psum(jnp.sum(expo, axis=1), 'cluster')  18.2 us
    pmax x1, blocking collectives, shards(): row_max = lax.pmax(jnp.max(scores, axis=1), 'cluster')  16.6 us
    dot_general x1, matrix products, shards(): lax.dot_general(lax.all_gather(documents, 'cluster', axis=1, tiled=True),...  15.1 us
    dot_general x1, matrix products, shards(): lax.dot_general(columns, shares, (((0,), (0,)), ((), ())), preferred_elem...  9.11 us
  transfers between devices with their start and end apart: 2, of which 2 were waited for; matrix products, arithmetic and copies ran while one was open for 0% of the time, Pallas kernels for 0%

profile of v2, /device:TPU:1, one launch (start us, length us, event | category | flops | bytes accessed | tf_op | source)
XLA Modules:
  0.0 408.4 jit_solution(780633393654426722)
XLA Ops:
  7.2 0.0 all-gather.2.cloned.1.call-start
  7.2 0.7 all-gather.2.cloned.1.call-update
  7.9 0.0 all-reduce.2.cloned.1.call-start
  7.9 1.9 reduce_sum.46
  9.9 77.0 %all-gather.2.cloned.1.call-done = bf16[2048,1024]{1,0:T(8,128)(2,1)} async-done(((bf16[2048,128]{1,0:T(8,128)(2,1)}), bf16[2048,1024]{1,0:T(8,128)(2,1)}) %all-gather.2.cloned.1.call-update) | async-done | bytes 4194320 | tf_op jit(solution)/shard_map/all_gather | solution.py:19
  86.9 15.1 %multiply_reduce_fusion = (f32[2048]{0:T(1024)S(1)}, f32[2048,2048]{0,1:T(8,128)}) fusion(bf16[2048,1024]{1,0:T(8,128)(2,1)} %all-gather.2.cloned.1.call-done, bf16[2048,1024]{1,0:T(8,128)(2,1)} %param.4), kind=kOutput, calls=%fused_computation.2 | convolution fusion | flops 8598321152 | bytes 25174016 | tf_op jit(solution)/shard_map/dot_general | solution.py:18
  102.0 16.6 %pmax.7 = f32[2048]{0:T(1024)S(1)} all-reduce(f32[2048]{0:T(1024)S(1)} %get-tuple-element.6), channel_id=1, replica_groups=mesh['cluster'=8,'dp'=16] {'cluster'}, use_global_device_ids=true, to_apply=%region_1.0 | all-reduce | flops 2048 | bytes 16384 | tf_op jit(solution)/shard_map/pmax | solution.py:26
  118.6 0.0 copy-start
  118.6 8.7 %fusion = f32[2048]{0:T(1024)S(1)} fusion(f32[2048,2048]{0,1:T(8,128)} %get-tuple-element.7, f32[2048]{0:T(1024)S(1)} %pmax.7), kind=kLoop, calls=%fused_computation.3 | loop fusion | flops 12580864 | bytes 16793600 | tf_op jit(solution)/shard_map/reduce_sum | solution.py:28
  127.3 18.2 %psum.35 = f32[2048]{0:T(1024)S(1)} all-reduce(f32[2048]{0:T(1024)S(1)} %fusion), channel_id=1, replica_groups=mesh['cluster'=8,'dp'=16] {'cluster'}, use_global_device_ids=true, to_apply=%region_3.0 | all-reduce | flops 2048 | bytes 16384 | tf_op jit(solution)/shard_map/psum | solution.py:28
  145.5 0.0 copy-done
  145.5 9.1 %fusion.1 = f32[2048,256]{1,0:T(8,128)} fusion(f32[2048,2048]{0,1:T(8,128)} %get-tuple-element.7, f32[2048]{0:T(1024)S(1)} %psum.35, f32[2048]{0:T(1024)S(1)} %pmax.7, f32[2048,256]{1,0:T(8,128)S(1)} %copy-done, f32[2048]{0:T(1024)S(1)} %reduce_sum.46), kind=kOutput, calls=%fused_computation.4 | convolution fusion | flops 2165309440 | bytes 20996096 | tf_op jit(solution)/shard_map/dot_general | solution.py:33
  154.6 0.0 all-reduce.2.cloned.1.call-update
  154.7 129.3 %all-reduce.2.cloned.1.call-done = f32[2048,256]{1,0:T(8,128)} async-done(((f32[2048,256]{1,0:T(8,128)}), f32[2048,256]{1,0:T(8,128)}) %all-reduce.2.cloned.1.call-update) | async-done | bytes 2097168 | tf_op jit(solution)/shard_map/psum | solution.py:32
  283.9 1.0 fusion.4
  284.9 20.4 %psum.37 = f32[256]{0:T(256)S(1)} all-reduce(f32[256]{0:T(256)S(1)} %get-tuple-element.3), channel_id=1, replica_groups=mesh['cluster'=8,'dp'=16] {'cluster'}, use_global_device_ids=true, to_apply=%region_8.0 | all-reduce | flops 256 | bytes 2048 | tf_op jit(solution)/shard_map/psum | solution.py:41
  305.3 32.0 %psum.38 = f32[256]{0:T(256)S(1)} all-reduce(f32[256]{0:T(256)S(1)} %psum.37), channel_id=1, replica_groups=mesh['cluster'=8,'dp'=16] {'dp'}, use_global_device_ids=true, to_apply=%region_9.0 | all-reduce | flops 256 | bytes 2048 | tf_op jit(solution)/shard_map/psum | solution.py:41
  337.3 2.3 multiply_reduce_fusion.1
  339.6 62.0 %psum.39 = f32[]{:T(128)} all-reduce(f32[]{:T(128)} %get-tuple-element.4), channel_id=1, replica_groups=mesh['cluster'=8,'dp'=16] {'cluster','dp'}, use_global_device_ids=true, to_apply=%region_11.0 | all-reduce | flops 1 | bytes 8 | tf_op jit(solution)/shard_map/psum | solution.py:43
Async XLA Ops:
  7.2 79.7 %all-gather.2.cloned.1.call-start = ((), (), s32[]{:S(2)}) async-start(), calls=%async_computation | async-start | bytes 4718592 | tf_op jit(solution)/shard_map/all_gather | solution.py:19
  7.9 276.0 %all-reduce.2.cloned.1.call-start = ((), (), s32[]{:S(2)}) async-start(), calls=%async_computation.1 | async-start | bytes 4194304 | tf_op jit(solution)/shard_map/psum | solution.py:32
  118.6 26.9 %copy-start = (f32[2048,256]{1,0:T(8,128)S(1)}, f32[2048,256]{1,0:T(8,128)}, u32[]{:S(2)}) copy-start(f32[2048,256]{1,0:T(8,128)} %param.5) | copy-start | bytes 6291460
Sparse Core Ops, SparseCore 0:
  10.2 76.6 all-gather.1
  154.8 129.0 all-reduce.1
